TPU v7x, 512 devices: a whole 4x8x8 slice. The times are simulated.
512 devices in a mesh: row: 8 (over y), col: 64 (over z, x, core).
Axes of the slice: x: 4, y: 8, z: 8, core: 2. Of those that a mesh axis runs over, the one named last changes fastest.
Arguments:
- sigma_top: bfloat16 [16384, 8, 64, 32], P('row', None, 'col'), as said below
- ancestor_rows: float32 [16384, 1024], P(('row', 'col')), may hold values from -0.0009765625 to 0.0009765625
- window_rows: float32 [1024, 1024], P('col'), may hold values from -0.1875 to 0.1875
- tile_inverse: float32 [4, 256, 256], replicated, as said below
- structure: int32 [4, 64], replicated, may hold values from 0 to 1, as said below
Outputs:
- cross_covariance: float32 [16384, 1024], P(('row', 'col'))
- window_covariance: float32 [1024, 1024], P('col')
Inputs may be any that keep to these rules, and one draw needn't show every extreme that they name: `sigma_top`: symmetric as an 16384 x 16384 matrix. `tile_inverse`: each tile is lower triangular. A tile in the structure of supernode j lies in the structure of every earlier supernode; supernode 0's structure holds every ancestor tile.
All inputs are finite; a program needn't handle non-finite values.
Results may differ from a plain program's by a relative error of at most 0.0013.
The roundings to bfloat16 on the way count: a program that leaves them out, or rounds other values in their place, can miss the bound.
Values may be sent and summed in bfloat16 or wider, within the bound.
No kernel may reach another device: no remote copies, remote signals or barrier semaphores. Data moves between devices by JAX's collectives and lax.ppermute only.
A program may use at most 64 MiB of HBM per device.

v0:
```python
import jax
import jax.numpy as jnp
from jax import lax
from jax.sharding import PartitionSpec as P


def lookup_rows(flags, tiles):
    matches = tiles[:, None] == jnp.arange(flags.shape[0], dtype=jnp.int32)[None, :]
    return jnp.sum(jnp.where(matches, flags[None, :], 0), axis=1).astype(jnp.float32)


def diagonal_total(partial_value):
    return lax.psum(partial_value, ("row", "col"))


def body(sigma_top, ancestor_rows, window_rows, tile_inverse, structure):
    highest = lax.Precision.HIGHEST
    supernodes = tile_inverse.shape[0]
    tile_width = tile_inverse.shape[1]
    window = supernodes * tile_width
    block_rows = sigma_top.shape[0]
    row_groups = sigma_top.shape[1]
    local_rows = ancestor_rows.shape[0]
    window_local = window_rows.shape[0]
    device_flat = lax.axis_index(("row", "col"))
    column_index = lax.axis_index("col")
    row_index = lax.axis_index("row")
    tiles_ancestor = (
        device_flat * local_rows + jnp.arange(local_rows, dtype=jnp.int32)
    ) // tile_width
    tiles_window = (
        column_index * window_local + jnp.arange(window_local, dtype=jnp.int32)
    ) // tile_width
    column_tiles = jnp.arange(window, dtype=jnp.int32) // tile_width
    upper_mask = column_tiles[None, :] > tiles_window[:, None]
    sigma_flat = sigma_top.reshape(block_rows, row_groups * local_rows)
    first_row = (row_index == 0).astype(jnp.float32)
    selections = [
        lookup_rows(structure[supernode], tiles_ancestor) for supernode in range(supernodes)
    ]
    cross = jnp.zeros((local_rows, window), jnp.float32)
    block = jnp.zeros((window_local, window), jnp.float32)
    for supernode in range(supernodes):
        left_edge = supernode * tile_width
        right_edge = left_edge + tile_width
        panel_product = jnp.dot(
            ancestor_rows[:, supernode * tile_width : (supernode + 1) * tile_width],
            tile_inverse[supernode],
            precision=highest,
            preferred_element_type=jnp.float32,
        )
        panel_anc = (selections[supernode][:, None] * panel_product).astype(jnp.bfloat16)
        keep = (tiles_window < supernode).astype(jnp.float32)
        product = jnp.dot(
            window_rows[:, supernode * tile_width : (supernode + 1) * tile_width],
            tile_inverse[supernode],
            precision=highest,
            preferred_element_type=jnp.float32,
        )
        panel_own = (keep[:, None] * product).astype(jnp.bfloat16)
        folded = lax.dot_general(
            sigma_flat,
            lax.all_gather(panel_anc, "col", axis=0, tiled=True),
            (((0,), (0,)), ((), ())),
            preferred_element_type=jnp.float32,
        )
        ancestor_part = lax.psum_scatter(
            folded.reshape(row_groups, local_rows, tile_width),
            "row",
            scatter_dimension=0,
            tiled=True,
        ).reshape(local_rows, tile_width)
        panel_all = lax.all_gather(panel_own, "col", axis=0, tiled=True)
        ancestor_f32 = panel_anc.astype(jnp.float32)
        own_f32 = panel_own.astype(jnp.float32)
        window_f32 = panel_all.astype(jnp.float32)
        result_ancestor = selections[supernode][:, None] * (
            ancestor_part
            + jnp.dot(cross, window_f32, precision=highest, preferred_element_type=jnp.float32)
        )
        diagonal_term = jnp.dot(
            ancestor_f32.T, result_ancestor, precision=highest, preferred_element_type=jnp.float32
        )
        if supernode > 0:
            upper = jnp.where(upper_mask, block, 0.0)
            upper_term = jnp.dot(
                upper, window_f32, precision=highest, preferred_element_type=jnp.float32
            )
            placed_term = lax.dynamic_update_slice_in_dim(
                jnp.zeros((window, tile_width), jnp.float32),
                upper_term,
                column_index * window_local,
                0,
            )
            window_term = jnp.dot(
                cross.T, ancestor_f32, precision=highest, preferred_element_type=jnp.float32
            )
            window_term = window_term + first_row * (
                jnp.dot(block.T, own_f32, precision=highest, preferred_element_type=jnp.float32)
                + placed_term
            )
            window_term = window_term[:left_edge]
            window_sum = lax.psum(window_term, ("row", "col"))
            diagonal_sum = diagonal_total(diagonal_term)
            result_window = jnp.concatenate(
                [window_sum, jnp.zeros((window - left_edge, tile_width), jnp.float32)], axis=0
            )
            window_part = jnp.dot(
                window_f32.T, result_window, precision=highest, preferred_element_type=jnp.float32
            )
            mine_result = lax.dynamic_slice_in_dim(
                result_window, column_index * window_local, window_local, 0
            )
        else:
            mine_result = jnp.zeros((window_local, tile_width), jnp.float32)
            window_part = jnp.zeros((tile_width, tile_width), jnp.float32)
            diagonal_sum = diagonal_total(diagonal_term)
        inverse = tile_inverse[supernode]
        diagonal = jnp.dot(
            inverse.T, inverse, precision=highest, preferred_element_type=jnp.float32
        )
        diagonal = diagonal + window_part + diagonal_sum
        placed = jnp.zeros((window, tile_width), jnp.float32).at[left_edge:right_edge].set(diagonal)
        mine_diagonal = lax.dynamic_slice_in_dim(
            placed, column_index * window_local, window_local, 0
        )
        row_tiles = tiles_window[:, None]
        column = jnp.where(
            row_tiles < supernode,
            -mine_result,
            jnp.where(row_tiles == supernode, mine_diagonal, 0.0),
        )
        cross = cross.at[:, left_edge:right_edge].set(-result_ancestor)
        block = block.at[:, left_edge:right_edge].set(column)
    return (cross, block)


def solution(mesh):
    placed = (P("row", None, "col", None), P(("row", "col"), None), P("col", None), P(), P())
    return jax.shard_map(
        body,
        mesh=mesh,
        in_specs=placed,
        out_specs=(P(("row", "col"), None), P("col", None)),
        check_vma=False,
    )
```

profile of v0, /device:TPU:23, one launch (start us, length us, event | category | flops | bytes accessed | tf_op | source)
XLA Modules:
  0.0 1614.0 jit_solution(3560617816976950300)
XLA Ops:
  7.3 0.7 copy-done.16
  8.0 0.2 select_reduce_fusion
  8.2 1.8 fusion.22
  10.2 1.8 fusion.23
  12.1 1.8 fusion.24
  13.9 84.5 %all-gather.5.cloned.1.call-done = bf16[2048,256]{1,0:T(8,128)(2,1)} async-done(((bf16[32,256]{1,0:T(8,128)(2,1)}), bf16[2048,256]{1,0:T(8,128)(2,1)}) %all-gather.5.cloned.1.call-update) | async-done | bytes 1048592 | tf_op jit(solution)/shard_map/all_gather | solution.py:63
  98.5 2.5 fusion.111
  101.0 0.8 fusion.25
  102.1 0.2 fusion.29
  102.3 52.7 %all_gather.25 = bf16[1024,256]{1,0:T(8,128)(2,1)} all-gather(bf16[16,256]{1,0:T(8,128)(2,1)S(1)} %fusion.29), channel_id=1, replica_groups=mesh['row'=8,'col'=64] {'col'}, dimensions={0}, use_global_device_ids=true | all-gather | bytes 532480 | tf_op jit(solution)/shard_map/all_gather | solution.py:73
  155.0 0.2 fusion.30
  155.3 49.1 %all_gather.27 = bf16[1024,256]{1,0:T(8,128)(2,1)S(1)} all-gather(bf16[16,256]{1,0:T(8,128)(2,1)S(1)} %fusion.30), channel_id=1, replica_groups=mesh['row'=8,'col'=64] {'col'}, dimensions={0}, use_global_device_ids=true | all-gather | bytes 532480 | tf_op jit(solution)/shard_map/all_gather | solution.py:73
  204.6 48.0 %all_gather.29 = bf16[1024,256]{1,0:T(8,128)(2,1)S(1)} all-gather(bf16[16,256]{1,0:T(8,128)(2,1)S(1)} %fusion.31), channel_id=1, replica_groups=mesh['row'=8,'col'=64] {'col'}, dimensions={0}, use_global_device_ids=true | all-gather | bytes 532480 | tf_op jit(solution)/shard_map/all_gather | solution.py:73
  252.8 54.0 %all_gather.31 = bf16[1024,256]{1,0:T(8,128)(2,1)} all-gather(bf16[16,256]{1,0:T(8,128)(2,1)S(1)} %fusion.32), channel_id=1, replica_groups=mesh['row'=8,'col'=64] {'col'}, dimensions={0}, use_global_device_ids=true | all-gather | bytes 532480 | tf_op jit(solution)/shard_map/all_gather | solution.py:73
  306.9 1.3 fusion.41
  308.2 2.4 fusion.112
  310.7 1.3 fusion.37
  312.0 2.4 fusion.113
  314.4 0.7 compare_reduce_fusion.2
  315.1 0.7 compare_reduce_fusion.1
  315.8 0.7 compare_reduce_fusion
  316.4 2.1 negate_select_fusion
  318.5 1.0 fusion.103
  319.6 70.1 %all-gather.11.cloned.1.call-done = bf16[2048,256]{1,0:T(8,128)(2,1)} async-done(((bf16[32,256]{1,0:T(8,128)(2,1)}), bf16[2048,256]{1,0:T(8,128)(2,1)}) %all-gather.11.cloned.1.call-update) | async-done | bytes 1048592 | tf_op jit(solution)/shard_map/all_gather | solution.py:63
  389.7 2.4 fusion.114
  392.1 0.6 copy-done.11
  392.8 1.6 fusion.60
  394.4 28.6 %reduce-scatter.7.cloned.1.call-done = f32[1,32,256]{2,1,0:T(8,128)} async-done(((f32[8,32,256]{2,1,0:T(8,128)}), f32[1,32,256]{2,1,0:T(8,128)}) %reduce-scatter.7.cloned.1.call-update) | async-done | bytes 32784 | tf_op jit(solution)/shard_map/reduce_scatter | solution.py:67
  422.9 1.7 select_dynamic-update-slice_fusion
  424.7 1.0 fusion.104
  425.7 1.6 fusion.105
  427.3 36.5 %reduce-scatter.9.cloned.1.call-done = f32[1,32,256]{2,1,0:T(8,128)} async-done(((f32[8,32,256]{2,1,0:T(8,128)}), f32[1,32,256]{2,1,0:T(8,128)}) %reduce-scatter.9.cloned.1.call-update) | async-done | bytes 32784 | tf_op jit(solution)/shard_map/reduce_scatter | solution.py:67
  463.8 1.1 fusion.19
  465.0 1.0 fusion.107
  466.0 277.6 %all-reduce.17.cloned.1.call-done = f32[256,256]{1,0:T(8,128)} async-done(((f32[256,256]{1,0:T(8,128)}), f32[256,256]{1,0:T(8,128)}) %all-reduce.17.cloned.1.call-update) | async-done | bytes 262160 | tf_op jit(solution)/shard_map/psum | solution.py:13
  743.6 1.5 convolution_add_fusion.1
  745.1 0.7 select_select_fusion
  745.8 0.6 fusion.65
  746.4 0.4 fusion.28
  746.8 1.7 slice_add_fusion.2
  748.6 0.6 fusion.67
  749.2 25.0 %reduce-scatter.11.cloned.1.call-done = f32[1,32,256]{2,1,0:T(8,128)} async-done(((f32[8,32,256]{2,1,0:T(8,128)}), f32[1,32,256]{2,1,0:T(8,128)}) %reduce-scatter.11.cloned.1.call-update) | async-done | bytes 32784 | tf_op jit(solution)/shard_map/reduce_scatter | solution.py:67
  774.2 1.4 fusion.18
  775.6 281.1 %all-reduce.23.cloned.1.call-done = (f32[256,256]{1,0:T(8,128)}, f32[256,256]{1,0:T(8,128)}) async-done(((f32[256,256]{1,0:T(8,128)}, f32[256,256]{1,0:T(8,128)}), (f32[256,256]{1,0:T(8,128)}, f32[256,256]{1,0:T(8,128)})) %all-reduce.23.cloned.1.call-update) | async-done | bytes 524304 | tf_op jit(solution)/shard_map/psum | solution.py:13
  1056.7 1.8 fusion.13
  1058.5 0.8 select_dynamic-update-slice_fusion.2
  1059.3 0.6 fusion.106
  1060.0 0.4 fusion.27
  1060.3 0.9 slice_add_fusion.1
  1061.3 0.3 all-reduce.19.cloned.1.call-start
  1061.5 0.4 copy-done.10
  1061.9 1.0 fusion.110
  1063.0 1.6 fusion.108
  1064.6 265.4 %all-reduce.21.cloned.1.call-done = (f32[256,256]{1,0:T(8,128)}, f32[512,256]{1,0:T(8,128)}) async-done(((f32[256,256]{1,0:T(8,128)}, f32[512,256]{1,0:T(8,128)}), (f32[256,256]{1,0:T(8,128)}, f32[512,256]{1,0:T(8,128)})) %all-reduce.21.cloned.1.call-update) | async-done | bytes 786448 | tf_op jit(solution)/shard_map/psum | solution.py:13
  1330.0 2.0 fusion.7
  1332.0 0.7 fusion.81
  1332.7 0.6 fusion.109
  1333.3 0.4 copy-done.2
  1333.7 0.4 fusion.26
  1334.1 1.0 slice_add_fusion
  1335.2 0.6 fusion.33
  1335.8 268.6 %all-reduce.19.cloned.1.call-done = (f32[256,256]{1,0:T(8,128)}, f32[768,256]{1,0:T(8,128)}) async-done(((f32[256,256]{1,0:T(8,128)}, f32[768,256]{1,0:T(8,128)}), (f32[256,256]{1,0:T(8,128)}, f32[768,256]{1,0:T(8,128)})) %all-reduce.19.cloned.1.call-update) | async-done | bytes 1048592 | tf_op jit(solution)/shard_map/psum | solution.py:13
  1604.4 2.0 fusion.16
  1606.5 0.6 copy-done.8
  (77 shorter events, 1.4 us)
Async XLA Ops:
  7.2 91.3 %copy-start = (bf16[2048,8,1,32]{0,3,2,1:T(8,128)(2,1)S(1)}, bf16[2048,8,1,32]{0,3,2,1:T(8,128)(2,1)}, u32[]{:S(2)}) copy-start(bf16[2048,8,1,32]{0,3,2,1:T(8,128)(2,1)} %param.29) | copy-start | bytes 3145732
  7.2 91.3 %all-gather.5.cloned.1.call-start = ((), (), s32[]{:S(2)}) async-start(), calls=%async_computation.4 | async-start | bytes 1064960 | tf_op jit(solution)/shard_map/all_gather | solution.py:63
  7.2 0.8 copy-start.16
  8.2 1.9 copy-start.14
  10.1 298.1 %all-gather.7.cloned.1.call-start = ((), (), s32[]{:S(2)}) async-start(), calls=%async_computation.6 | async-start | bytes 1064960 | tf_op jit(solution)/shard_map/all_gather | solution.py:63
  12.0 300.0 %all-gather.9.cloned.1.call-start = ((), (), s32[]{:S(2)}) async-start(), calls=%async_computation.8 | async-start | bytes 1064960 | tf_op jit(solution)/shard_map/all_gather | solution.py:63
  13.9 302.6 %reduce-scatter.5.cloned.1.call-start = ((), (), s32[]{:S(2)}) async-start(), calls=%async_computation.5 | async-start | bytes 294912 | tf_op jit(solution)/shard_map/reduce_scatter | solution.py:67
  98.5 2.6 copy-start.1
  101.0 288.7 %all-gather.11.cloned.1.call-start = ((), (), s32[]{:S(2)}) async-start(), calls=%async_computation.10 | async-start | bytes 1064960 | tf_op jit(solution)/shard_map/all_gather | solution.py:63
  101.0 1.0 copy-start.15
  101.9 321.0 %reduce-scatter.7.cloned.1.call-start = ((), (), s32[]{:S(2)}) async-start(), calls=%async_computation.7 | async-start | bytes 294912 | tf_op jit(solution)/shard_map/reduce_scatter | solution.py:67
  310.6 153.2 %reduce-scatter.9.cloned.1.call-start = ((), (), s32[]{:S(2)}) async-start(), calls=%async_computation.9 | async-start | bytes 294912 | tf_op jit(solution)/shard_map/reduce_scatter | solution.py:67
  314.4 429.2 %all-reduce.17.cloned.1.call-start = ((), (), s32[]{:S(2)}) async-start(), calls=%async_computation.12 | async-start | bytes 524288 | tf_op jit(solution)/shard_map/psum | solution.py:13
  316.4 2.1 copy-start.13
  319.6 454.6 %reduce-scatter.11.cloned.1.call-start = ((), (), s32[]{:S(2)}) async-start(), calls=%async_computation.11 | async-start | bytes 294912 | tf_op jit(solution)/shard_map/reduce_scatter | solution.py:67
  392.0 0.7 copy-start.11
  392.1 664.6 %all-reduce.23.cloned.1.call-start = ((), (), s32[]{:S(2)}) async-start(), calls=%async_computation.15 | async-start | bytes 1048576 | tf_op jit(solution)/shard_map/psum | solution.py:13
  424.7 1.1 copy-start.12
  748.5 581.4 %all-reduce.21.cloned.1.call-start = ((), (), s32[]{:S(2)}) async-start(), calls=%async_computation.14 | async-start | bytes 1572864 | tf_op jit(solution)/shard_map/psum | solution.py:13
  1056.7 1.8 copy-start.9
  1058.5 1.8 copy-start.6
  1061.2 0.7 copy-start.10
  1061.3 543.2 %all-reduce.19.cloned.1.call-start = ((), (), s32[]{:S(2)}) async-start(), calls=%async_computation.13 | async-start | bytes 2097152 | tf_op jit(solution)/shard_map/psum | solution.py:13
  1330.0 2.0 copy-start.7
  1332.7 1.0 copy-start.2
  1332.7 1.4 copy-start.4
  1335.8 270.7 %copy-start.3 = (f32[32,1024]{1,0:T(8,128)}, f32[32,1024]{1,0:T(8,128)S(1)}, u32[]{:S(2)}) copy-start(f32[32,1024]{1,0:T(8,128)S(1)} %negate_dynamic-update-slice_fusion) | copy-start | bytes 393220
  1604.4 2.0 copy-start.5
  1606.5 0.6 copy-start.8
Sparse Core Ops, SparseCore 0:
  11.9 86.4 all-gather.4
  102.4 79.7 all-gather.6
  185.5 79.7 all-gather.8
  268.0 30.7 reduce-scatter.4
  302.6 87.0 all-gather.10
  392.5 30.3 reduce-scatter.6
  425.7 38.0 reduce-scatter.8
  469.6 273.9 all-reduce.16
  746.4 27.7 reduce-scatter.10
  780.1 276.5 all-reduce.22
  1061.9 268.0 all-reduce.20
  1335.3 269.0 all-reduce.18
where the time goes:
time: 1610 us
  waiting for transfers between devices  1340 us (83%)
  blocking collectives  204 us (13%)
  matrix products  45.4 us (3%)
    psum x4, waiting for transfers between devices, diagonal_total(): return lax.psum(partial_value, ('row', 'col'))  1090 us
    all_gather x4, blocking collectives, body(): panel_all = lax.all_gather(panel_own, 'col', axis=0, tiled=True)  204 us
    all_gather x4, waiting for transfers between devices, body(): lax.all_gather(panel_anc, 'col', axis=0, tiled=True)  155 us
    reduce_scatter x4, waiting for transfers between devices, body(): lax.psum_scatter(folded.reshape(row_groups, local_rows, tile_width), 'row...  90 us
  transfers between devices with their start and end apart: 12, of which 9 were waited for; matrix products, arithmetic and copies ran while one was open for 3% of the time, Pallas kernels for 0%

commit v1 on v0

--- a/solution.py
+++ b/solution.py
@@ -2,6 +2,11 @@
 import jax.numpy as jnp
 from jax import lax
 from jax.sharding import PartitionSpec as P
+
+
+def gather_by_exchange(value, axis, dim):
+    copies = jnp.concatenate([value] * lax.axis_size(axis), axis=dim)
+    return lax.all_to_all(copies, axis, dim, dim, tiled=True)
 
 
 def lookup_rows(flags, tiles):
@@ -60,7 +65,7 @@
         panel_own = (keep[:, None] * product).astype(jnp.bfloat16)
         folded = lax.dot_general(
             sigma_flat,
-            lax.all_gather(panel_anc, "col", axis=0, tiled=True),
+            gather_by_exchange(panel_anc, "col", 0),
             (((0,), (0,)), ((), ())),
             preferred_element_type=jnp.float32,
         )

time: 1610 us -> 1600 us (level)
  waiting for transfers between devices: 1340 us -> 1230 us
  starting transfers between devices: 0.72 us -> 42.2 us
  local copies, waits for them, and re-layouts: 2.93 us -> 42.4 us
    all_gather x4 -> x0, waiting for transfers between devices: 155 us -> none  [body(): lax.all_gather(panel_anc, 'col', axis=0, tiled=True)]
    all_to_all x0 -> x4, starting transfers between devices: none -> 41.7 us  [gather_by_exchange(): return lax.all_to_all(copies, axis, dim, dim, tiled=True)]
    unnamed x34 -> x282, local copies, waits for them, and re-layouts: 2.91 us -> 41.7 us
    reduce_scatter x4, waiting for transfers between devices: 90 us -> 120 us  [body(): lax.psum_scatter(folded.reshape(row_groups, local_rows, tile_width), 'row...]
  transfers between devices with their start and end apart: 12 -> 12, of which waited for: 9 -> 9; matrix products, arithmetic and copies ran while one was open for 3% -> 5% of each run, Pallas kernels for 0% -> 0%
where the time goes in v1:
time: 1600 us
  waiting for transfers between devices  1230 us (77%)
  blocking collectives  219 us (14%)
  local copies, waits for them, and re-layouts  42.4 us (3%)
  starting transfers between devices  42.2 us (3%)
  matrix products  41.6 us (3%)
  between operations  16.1 us (1%)
    psum x4, waiting for transfers between devices, diagonal_total(): return lax.psum(partial_value, ('row', 'col'))  1090 us
    all_gather x4, blocking collectives, body(): panel_all = lax.all_gather(panel_own, 'col', axis=0, tiled=True)  219 us
    reduce_scatter x4, waiting for transfers between devices, body(): lax.psum_scatter(folded.reshape(row_groups, local_rows, tile_width), 'row...  120 us
    unnamed x282, local copies, waits for them, and re-layouts  41.7 us
    all_to_all x4, starting transfers between devices, gather_by_exchange(): return lax.all_to_all(copies, axis, dim, dim, tiled=True)  41.7 us
  transfers between devices with their start and end apart: 12, of which 9 were waited for; matrix products, arithmetic and copies ran while one was open for 5% of the time, Pallas kernels for 0%

profile of v1, /device:TPU:23, one launch (start us, length us, event | category | flops | bytes accessed | tf_op | source)
XLA Modules:
  0.0 1599.6 jit_solution(14770461197538024939)
XLA Ops:
  7.2 0.7 copy-done.16
  8.2 1.2 constant_dynamic-update-slice_fusion.63
  10.1 1.0 copy-done.10
  11.1 14.3 all-to-all-start
  27.5 0.9 constant_dynamic-update-slice_fusion.255
  32.0 0.6 constant_dynamic-update-slice_fusion.248
  37.4 0.6 constant_dynamic-update-slice_fusion.239
  44.0 0.6 constant_dynamic-update-slice_fusion.228
  46.5 0.6 constant_dynamic-update-slice_fusion.224
  52.5 1.0 copy-done.3
  53.4 10.5 all-to-all-start.1
  65.1 0.6 constant_dynamic-update-slice_fusion.212
  65.7 0.6 constant_dynamic-update-slice_fusion.211
  74.7 16.1 %all-to-all-done.1 = bf16[64,32,256]{2,1,0:T(8,128)(2,1)} async-done(((bf16[64,32,256]{2,1,0:T(8,128)(2,1)}), bf16[64,32,256]{2,1,0:T(8,128)(2,1)}, u32[]{:S(2)}, u32[]{:S(2)}) %all-to-all-start.1) | async-done | bytes 1048608 | tf_op jit(solution)/shard_map/all_to_all | solution.py:9
  90.8 7.6 all-to-all-start.2
  98.5 0.6 constant_dynamic-update-slice_fusion.196
  99.1 0.6 constant_dynamic-update-slice_fusion.195
  101.7 69.1 %all_gather.12 = bf16[1024,256]{1,0:T(8,128)(2,1)} all-gather(bf16[16,256]{1,0:T(8,128)(2,1)S(1)} %fusion.29), channel_id=1, replica_groups=mesh['row'=8,'col'=64] {'col'}, dimensions={0}, use_global_device_ids=true | all-gather | bytes 532480 | tf_op jit(solution)/shard_map/all_gather | solution.py:78
  171.1 48.0 %all_gather.13 = bf16[1024,256]{1,0:T(8,128)(2,1)S(1)} all-gather(bf16[16,256]{1,0:T(8,128)(2,1)S(1)} %fusion.30), channel_id=1, replica_groups=mesh['row'=8,'col'=64] {'col'}, dimensions={0}, use_global_device_ids=true | all-gather | bytes 532480 | tf_op jit(solution)/shard_map/all_gather | solution.py:78
  219.3 49.4 %all_gather.14 = bf16[1024,256]{1,0:T(8,128)(2,1)S(1)} all-gather(bf16[16,256]{1,0:T(8,128)(2,1)S(1)} %fusion.31), channel_id=1, replica_groups=mesh['row'=8,'col'=64] {'col'}, dimensions={0}, use_global_device_ids=true | all-gather | bytes 532480 | tf_op jit(solution)/shard_map/all_gather | solution.py:78
  268.9 52.5 %all_gather.15 = bf16[1024,256]{1,0:T(8,128)(2,1)} all-gather(bf16[16,256]{1,0:T(8,128)(2,1)S(1)} %fusion.32), channel_id=1, replica_groups=mesh['row'=8,'col'=64] {'col'}, dimensions={0}, use_global_device_ids=true | all-gather | bytes 532480 | tf_op jit(solution)/shard_map/all_gather | solution.py:78
  321.5 9.3 all-to-all-start.3
  330.8 2.4 fusion.111
  333.3 1.3 fusion.41
  334.6 2.4 fusion.112
  337.1 1.3 fusion.37
  338.4 2.4 fusion.113
  340.8 0.6 compare_reduce_fusion.2
  341.5 0.6 compare_reduce_fusion.1
  342.1 0.7 compare_reduce_fusion
  342.8 26.1 %reduce-scatter.5.cloned.1.call-done = f32[1,32,256]{2,1,0:T(8,128)} async-done(((f32[8,32,256]{2,1,0:T(8,128)}), f32[1,32,256]{2,1,0:T(8,128)}) %reduce-scatter.5.cloned.1.call-update) | async-done | bytes 32784 | tf_op jit(solution)/shard_map/reduce_scatter | solution.py:72
  368.8 2.1 negate_select_fusion
  370.9 1.0 fusion.103
  372.0 2.4 fusion.114
  374.7 1.6 fusion.60
  376.3 32.6 %reduce-scatter.7.cloned.1.call-done = f32[1,32,256]{2,1,0:T(8,128)} async-done(((f32[8,32,256]{2,1,0:T(8,128)}), f32[1,32,256]{2,1,0:T(8,128)}) %reduce-scatter.7.cloned.1.call-update) | async-done | bytes 32784 | tf_op jit(solution)/shard_map/reduce_scatter | solution.py:72
  408.9 1.8 select_dynamic-update-slice_fusion
  410.7 1.0 fusion.104
  411.7 1.6 fusion.105
  413.3 36.6 %reduce-scatter.9.cloned.1.call-done = f32[1,32,256]{2,1,0:T(8,128)} async-done(((f32[8,32,256]{2,1,0:T(8,128)}), f32[1,32,256]{2,1,0:T(8,128)}) %reduce-scatter.9.cloned.1.call-update) | async-done | bytes 32784 | tf_op jit(solution)/shard_map/reduce_scatter | solution.py:72
  449.9 1.1 fusion.19
  451.0 1.0 fusion.107
  452.0 277.5 %all-reduce.17.cloned.1.call-done = f32[256,256]{1,0:T(8,128)} async-done(((f32[256,256]{1,0:T(8,128)}), f32[256,256]{1,0:T(8,128)}) %all-reduce.17.cloned.1.call-update) | async-done | bytes 262160 | tf_op jit(solution)/shard_map/psum | solution.py:18
  729.5 1.5 convolution_add_fusion.1
  731.0 0.7 select_select_fusion
  732.7 1.7 slice_add_fusion.2
  734.5 0.6 fusion.67
  735.1 24.8 %reduce-scatter.11.cloned.1.call-done = f32[1,32,256]{2,1,0:T(8,128)} async-done(((f32[8,32,256]{2,1,0:T(8,128)}), f32[1,32,256]{2,1,0:T(8,128)}) %reduce-scatter.11.cloned.1.call-update) | async-done | bytes 32784 | tf_op jit(solution)/shard_map/reduce_scatter | solution.py:72
  760.0 1.4 fusion.18
  761.4 281.0 %all-reduce.23.cloned.1.call-done = (f32[256,256]{1,0:T(8,128)}, f32[256,256]{1,0:T(8,128)}) async-done(((f32[256,256]{1,0:T(8,128)}, f32[256,256]{1,0:T(8,128)}), (f32[256,256]{1,0:T(8,128)}, f32[256,256]{1,0:T(8,128)})) %all-reduce.23.cloned.1.call-update) | async-done | bytes 524304 | tf_op jit(solution)/shard_map/psum | solution.py:18
  1042.4 1.8 fusion.13
  1044.2 0.8 select_dynamic-update-slice_fusion.2
  1045.0 0.6 fusion.106
  1046.0 0.9 slice_add_fusion.1
  1047.0 1.0 fusion.110
  1048.0 1.6 fusion.108
  1049.7 266.0 %all-reduce.21.cloned.1.call-done = (f32[256,256]{1,0:T(8,128)}, f32[512,256]{1,0:T(8,128)}) async-done(((f32[256,256]{1,0:T(8,128)}, f32[512,256]{1,0:T(8,128)}), (f32[256,256]{1,0:T(8,128)}, f32[512,256]{1,0:T(8,128)})) %all-reduce.21.cloned.1.call-update) | async-done | bytes 786448 | tf_op jit(solution)/shard_map/psum | solution.py:18
  1315.6 2.0 fusion.7
  1317.6 0.7 fusion.81
  1318.4 0.6 fusion.109
  1319.8 1.0 slice_add_fusion
  1321.5 268.6 %all-reduce.19.cloned.1.call-done = (f32[256,256]{1,0:T(8,128)}, f32[768,256]{1,0:T(8,128)}) async-done(((f32[256,256]{1,0:T(8,128)}, f32[768,256]{1,0:T(8,128)}), (f32[256,256]{1,0:T(8,128)}, f32[768,256]{1,0:T(8,128)})) %all-reduce.19.cloned.1.call-update) | async-done | bytes 1048592 | tf_op jit(solution)/shard_map/psum | solution.py:18
  1590.0 2.0 fusion.16
  1592.2 0.6 copy-done.9
  (325 shorter events, 38.9 us)
Async XLA Ops:
  7.2 323.7 %copy-start = (bf16[2048,8,1,32]{0,3,2,1:T(8,128)(2,1)S(1)}, bf16[2048,8,1,32]{0,3,2,1:T(8,128)(2,1)}, u32[]{:S(2)}) copy-start(bf16[2048,8,1,32]{0,3,2,1:T(8,128)(2,1)} %param.29) | copy-start | bytes 3145732
  7.2 0.8 copy-start.16
  10.1 1.0 copy-start.10
  11.1 14.3 copy-start.1
  11.1 14.3 copy-start.14
  11.1 41.3 %all-to-all-start = ((bf16[64,32,256]{2,1,0:T(8,128)(2,1)}), bf16[64,32,256]{2,1,0:T(8,128)(2,1)S(1)}, u32[]{:S(2)}, u32[]{:S(2)}) async-start(bf16[64,32,256]{2,1,0:T(8,128)(2,1)} %bitcast.116), calls=%async_computation | async-start | bytes 2097152 | tf_op jit(solution)/shard_map/all_to_all | solution.py:9
  26.4 1.0 copy-start.11
  27.5 24.4 %copy-start.12 = (bf16[2048,256]{1,0:T(8,128)(2,1)}, bf16[2048,256]{1,0:T(8,128)(2,1)S(1)}, u32[]{:S(2)}) copy-start(bf16[2048,256]{1,0:T(8,128)(2,1)S(1)} %constant_dynamic-update-slice_fusion.128) | copy-start | bytes 3145732
  52.5 1.0 copy-start.3
  53.4 37.4 %all-to-all-start.1 = ((bf16[64,32,256]{2,1,0:T(8,128)(2,1)}), bf16[64,32,256]{2,1,0:T(8,128)(2,1)}, u32[]{:S(2)}, u32[]{:S(2)}) async-start(bf16[64,32,256]{2,1,0:T(8,128)(2,1)} %bitcast.117), calls=%async_computation.2 | async-start | bytes 2097152 | tf_op jit(solution)/shard_map/all_to_all | solution.py:9
  90.8 230.6 %all-to-all-start.2 = ((bf16[64,32,256]{2,1,0:T(8,128)(2,1)}), bf16[64,32,256]{2,1,0:T(8,128)(2,1)}, u32[]{:S(2)}, u32[]{:S(2)}) async-start(bf16[64,32,256]{2,1,0:T(8,128)(2,1)} %bitcast.118), calls=%async_computation.4 | async-start | bytes 2097152 | tf_op jit(solution)/shard_map/all_to_all | solution.py:9
  99.1 2.4 copy-start.15
  321.5 50.5 %all-to-all-start.3 = ((bf16[64,32,256]{2,1,0:T(8,128)(2,1)}), bf16[64,32,256]{2,1,0:T(8,128)(2,1)}, u32[]{:S(2)}, u32[]{:S(2)}) async-start(bf16[64,32,256]{2,1,0:T(8,128)(2,1)} %bitcast.24), calls=%async_computation.6 | async-start | bytes 2097152 | tf_op jit(solution)/shard_map/all_to_all | solution.py:9
  330.8 38.0 %reduce-scatter.5.cloned.1.call-start = ((), (), s32[]{:S(2)}) async-start(), calls=%async_computation.8 | async-start | bytes 294912 | tf_op jit(solution)/shard_map/reduce_scatter | solution.py:72
  333.2 75.6 %reduce-scatter.7.cloned.1.call-start = ((), (), s32[]{:S(2)}) async-start(), calls=%async_computation.9 | async-start | bytes 294912 | tf_op jit(solution)/shard_map/reduce_scatter | solution.py:72
  337.0 112.9 %reduce-scatter.9.cloned.1.call-start = ((), (), s32[]{:S(2)}) async-start(), calls=%async_computation.10 | async-start | bytes 294912 | tf_op jit(solution)/shard_map/reduce_scatter | solution.py:72
  340.7 388.8 %all-reduce.17.cloned.1.call-start = ((), (), s32[]{:S(2)}) async-start(), calls=%async_computation.12 | async-start | bytes 524288 | tf_op jit(solution)/shard_map/psum | solution.py:18
  371.9 388.0 %reduce-scatter.11.cloned.1.call-start = ((), (), s32[]{:S(2)}) async-start(), calls=%async_computation.11 | async-start | bytes 294912 | tf_op jit(solution)/shard_map/reduce_scatter | solution.py:72
  374.4 668.0 %all-reduce.23.cloned.1.call-start = ((), (), s32[]{:S(2)}) async-start(), calls=%async_computation.15 | async-start | bytes 1048576 | tf_op jit(solution)/shard_map/psum | solution.py:18
  734.5 581.2 %all-reduce.21.cloned.1.call-start = ((), (), s32[]{:S(2)}) async-start(), calls=%async_computation.14 | async-start | bytes 1572864 | tf_op jit(solution)/shard_map/psum | solution.py:18
  1042.4 1.8 copy-start.13
  1044.2 1.8 copy-start.7
  1046.9 543.1 %all-reduce.19.cloned.1.call-start = ((), (), s32[]{:S(2)}) async-start(), calls=%async_computation.13 | async-start | bytes 2097152 | tf_op jit(solution)/shard_map/psum | solution.py:18
  1315.6 2.0 copy-start.8
  1318.4 1.0 copy-start.2
  1318.4 1.4 copy-start.5
  1321.4 270.6 %copy-start.4 = (f32[32,1024]{1,0:T(8,128)}, f32[32,1024]{1,0:T(8,128)S(1)}, u32[]{:S(2)}) copy-start(f32[32,1024]{1,0:T(8,128)S(1)} %negate_dynamic-update-slice_fusion) | copy-start | bytes 393220
  1590.0 2.0 copy-start.6
  1592.2 0.6 copy-start.9
Sparse Core Ops, SparseCore 0:
  334.4 34.3 reduce-scatter.4
  371.8 37.0 reduce-scatter.6
  411.7 38.1 reduce-scatter.8
  455.5 273.9 all-reduce.16
  732.1 27.7 reduce-scatter.10
  765.8 276.4 all-reduce.22
  1047.5 268.0 all-reduce.20
  1320.9 269.0 all-reduce.18
